TPU v7x, 32 devices: a whole 2x2x4 slice. The times are simulated.
32 devices in a mesh: grp: 2 (over y), blk: 4 (over z), rep: 2 (over x), sub: 2 (over core).
Axes of the slice: x: 2, y: 2, z: 4, core: 2. Of those that a mesh axis runs over, the one named last changes fastest.
Arguments:
- image_feature_vectors: float32 [16384, 768], P(('grp', 'blk', 'rep', 'sub')), parts along dimension 0
- centroid_group_label: int32 [16384], P(('grp', 'blk', 'rep', 'sub')), parts along dimension 0, may hold values from 0 to 23, as said below
- group_member_sizes: int32 [48], P('grp'), parts along dimension 0, may hold values from 32 to 512, as said below
- softmax_heat_factors: float32 [48], P('grp'), parts along dimension 0, may hold values from 0.1 to 1
Outputs:
- scores: float32 [16384], P(('grp', 'blk', 'rep', 'sub')), parts along dimension 0
There are 2 independent parts, one for each index of `grp`. A program takes and returns all parts, laid end to end along the dimension named above; each array names one. Nothing has to cross between parts.
Inputs may be any that keep to these rules, and one draw needn't show every extreme that they name: `centroid_group_label`: cluster c belongs to owner c // 3, owners being numbered over (blk, rep) with blk slowest. The rows of cluster c number exactly group_member_sizes[c]. Every owner's clusters hold 1024 rows together. Each device holds at most 96 rows of the clusters of one owner, exactly 96 for some owner; the devices that share one sub index hold exactly 512 rows of each owner's clusters together. `group_member_sizes`: one cluster of every owner holds exactly 512 rows.
All inputs are finite; a program needn't handle non-finite values.
Results may differ from a plain program's by a relative error of at most 0.0003.
Values may be sent and summed in bfloat16 or wider, within the bound.
A program may use at most 64 MiB of HBM per device.

v0:
```python
import functools

import jax
import jax.numpy as jnp
from jax import lax
from jax.experimental import pallas as pl
from jax.experimental.pallas import tpu as pltpu
from jax.sharding import PartitionSpec as P

D = 768
GROUPS_EACH_PEER = 3
MESH = pl.DeviceIdType.MESH
F32 = jnp.float32
BF16 = jnp.bfloat16


def kernel(
    n_blk, n_rep, n_sub, slots,
    x_ref, label_ref, sizes_ref, heats_ref, out_ref,
    unit, out_rows, out_tags, rows, tags, back_out, back_in,
    row_send, row_recv, tag_send, tag_recv, fwd_send, fwd_recv,
    fwd_tag_send, fwd_tag_recv, back_send, back_recv,
):
    owners = n_blk * n_rep
    count = x_ref.shape[0]
    me = lax.axis_index("blk") * n_rep + lax.axis_index("rep")
    sub = lax.axis_index("sub")

    def device(owner):
        return {"blk": owner // n_rep, "rep": owner % n_rep}

    sibling = {"sub": 1 - sub}

    def peers(body):
        def step(k, carry):
            body(k, lax.rem(me + k, owners))
            return carry

        lax.fori_loop(1, owners, step, 0, unroll=owners <= 16)

    barrier = pltpu.get_barrier_semaphore()
    peers(lambda k, o: pl.semaphore_signal(barrier, inc=1, device_id=device(o), device_id_type=MESH))
    pl.semaphore_signal(barrier, inc=1, device_id=sibling, device_id_type=MESH)

    labels = label_ref[...]
    owner_range = lax.broadcasted_iota(jnp.int32, (owners, count), 0) * GROUPS_EACH_PEER
    local = labels - owner_range
    mine_owner = (local >= 0) & (local < GROUPS_EACH_PEER)
    upper = (
        lax.broadcasted_iota(jnp.int32, (count, count), 0)
        < lax.broadcasted_iota(jnp.int32, (count, count), 1)
    )
    before = jnp.dot(
        jnp.where(mine_owner, 1.0, 0.0).astype(BF16),
        jnp.where(upper, 1.0, 0.0).astype(BF16),
        preferred_element_type=F32,
    )
    rank = jnp.sum(jnp.where(mine_owner, before, 0.0), axis=0, keepdims=True).astype(jnp.int32)
    first = jnp.sum(jnp.where(mine_owner, owner_range, 0), axis=0, keepdims=True)
    member = labels - first
    code = first * 256 + rank
    slot_range = lax.broadcasted_iota(jnp.int32, (slots, count), 0)
    wide_range = lax.broadcasted_iota(jnp.int32, (128, count), 0)
    member_hot = jnp.where(
        lax.broadcasted_iota(jnp.int32, (8, count), 0) == member, 1.0, 0.0
    ).astype(BF16)

    def picked(owner, span):
        return jnp.where(span + owner * (GROUPS_EACH_PEER * 256) == code, 1.0, 0.0).astype(BF16)

    def tags_for(owner):
        return lax.dot_general(
            member_hot, picked(owner, wide_range), (((1,), (1,)), ((), ())),
            preferred_element_type=F32,
        )

    def rows_for(owner):
        return jnp.dot(
            picked(owner, slot_range), unit[...], preferred_element_type=F32
        ).astype(BF16)

    x = x_ref[...]
    squares = jnp.sum(x * x, axis=1, keepdims=True)
    unit[...] = (x * lax.rsqrt(squares + 1e-06)).astype(BF16)

    pl.semaphore_wait(barrier, owners)

    def row_copy(o, slot):
        return pltpu.make_async_remote_copy(
            src_ref=out_rows.at[o], dst_ref=rows.at[0, slot],
            send_sem=row_send.at[o], recv_sem=row_recv.at[slot],
            device_id=device(o), device_id_type=MESH,
        )

    def tag_copy(o, slot):
        return pltpu.make_async_remote_copy(
            src_ref=out_tags.at[o], dst_ref=tags.at[0, slot],
            send_sem=tag_send.at[o], recv_sem=tag_recv.at[slot],
            device_id=device(o), device_id_type=MESH,
        )

    def back_copy(o, slot):
        return pltpu.make_async_remote_copy(
            src_ref=back_out.at[o], dst_ref=back_in.at[slot],
            send_sem=back_send.at[o], recv_sem=back_recv.at[slot],
            device_id=device(o), device_id_type=MESH,
        )

    def forward(o):
        return pltpu.make_async_remote_copy(
            src_ref=rows.at[0, o], dst_ref=rows.at[1, o],
            send_sem=fwd_send.at[o], recv_sem=fwd_recv.at[o],
            device_id=sibling, device_id_type=MESH,
        )

    def send(k, o):
        out_tags[o] = tags_for(o)
        tag_copy(o, me).start()
        out_rows[o] = rows_for(o)
        row_copy(o, me).start()

    peers(send)
    tags[0, me] = tags_for(me)
    rows[0, me] = rows_for(me)
    forward(me).start()

    def source(k):
        return lax.rem(me - k + owners, owners)

    def arrive(k, o):
        o = source(k)
        row_copy(o, o).wait_recv()
        forward(o).start()

    def arrive_tag(k, o):
        o = source(k)
        tag_copy(o, o).wait_recv()

    peers(arrive_tag)
    forward_tags = pltpu.make_async_remote_copy(
        src_ref=tags.at[0], dst_ref=tags.at[1],
        send_sem=fwd_tag_send, recv_sem=fwd_tag_recv,
        device_id=sibling, device_id_type=MESH,
    )
    forward_tags.start()

    hot = jnp.concatenate([tags[0, o][:, :slots] for o in range(owners)], axis=1)
    heat = jnp.zeros_like(hot[0:1])
    size = jnp.zeros_like(heat)
    for g in range(GROUPS_EACH_PEER):
        at = me * GROUPS_EACH_PEER + g
        heat = heat + hot[g : g + 1] * heats_ref[at]
        size = jnp.where(hot[g : g + 1] > 0.5, sizes_ref[at].astype(F32), size)
    valid = heat > 0.0
    inverse = 1.0 / jnp.where(valid, heat, 1.0)
    offset = inverse - jnp.log(jnp.where(valid, size, 1.0))
    hot = hot.astype(BF16)

    peers(arrive)
    forward_tags.wait_recv()

    own = rows[0].reshape(owners * slots, D)

    def column(s, o):
        cosine = lax.dot_general(
            rows[s, o], own, (((1,), (1,)), ((), ())), preferred_element_type=F32
        )
        same = lax.dot_general(
            tags[s, o][:, :slots].astype(BF16), hot, (((0,), (0,)), ((), ())),
            preferred_element_type=F32,
        )
        weight = jnp.exp((cosine - 1.0) * inverse) * same
        return jnp.sum(weight, axis=0, keepdims=True)

    total = jnp.zeros((1, owners * slots), F32)
    total = lax.fori_loop(0, owners, lambda o, t: t + column(0, o), total)

    def other(k, t):
        o = lax.rem(1 * me + k, owners)
        forward(o).wait_recv()
        return t + column(1, o)

    total = lax.fori_loop(0, owners, other, total)
    scores = jnp.where(valid, offset + jnp.log(jnp.where(valid, total, 1.0)), 0.0)
    for o in range(owners):
        back_out[o] = jnp.zeros((8, 128), F32)
        back_out[o, 0:1, 0:slots] = scores[:, o * slots : (o + 1) * slots]
    back_in[me] = back_out[me]

    peers(lambda k, o: back_copy(o, me).start())

    def drain(k, o):
        tag_copy(o, me).wait_send()
        row_copy(o, me).wait_send()
        forward(o).wait_send()

    peers(drain)
    forward(me).wait_send()
    forward_tags.wait_send()

    def arrive_back(k, o):
        back_copy(source(k), source(k)).wait_recv()

    peers(arrive_back)
    table = back_in[:, 0, :]
    spread = jnp.where(wide_range == rank, 1.0, 0.0)
    found = jnp.dot(table, spread, precision=lax.Precision.HIGHEST, preferred_element_type=F32)
    out_ref[...] = jnp.sum(jnp.where(mine_owner, found, 0.0), axis=0, keepdims=True)
    peers(lambda k, o: back_copy(o, me).wait_send())


def on_device(vectors, labels, sizes, heats):
    count = vectors.shape[0]
    n_blk, n_rep, n_sub = (lax.axis_size(a) for a in ("blk", "rep", "sub"))
    owners = n_blk * n_rep
    share = count // owners
    slots = -(-(share + share // 2) // 16) * 16
    dma = pltpu.SemaphoreType.DMA
    out = pl.pallas_call(
        functools.partial(kernel, n_blk, n_rep, n_sub, slots),
        out_shape=jax.ShapeDtypeStruct((1, count), F32),
        in_specs=[
            pl.BlockSpec(memory_space=pltpu.VMEM),
            pl.BlockSpec(memory_space=pltpu.VMEM),
            pl.BlockSpec(memory_space=pltpu.SMEM),
            pl.BlockSpec(memory_space=pltpu.SMEM),
        ],
        out_specs=pl.BlockSpec(memory_space=pltpu.VMEM),
        scratch_shapes=[
            pltpu.VMEM((count, D), BF16),
            pltpu.VMEM((owners, slots, D), BF16),
            pltpu.VMEM((owners, 8, 128), F32),
            pltpu.VMEM((n_sub, owners, slots, D), BF16),
            pltpu.VMEM((n_sub, owners, 8, 128), F32),
            pltpu.VMEM((owners, 8, 128), F32),
            pltpu.VMEM((owners, 8, 128), F32),
            dma((owners,)), dma((owners,)), dma((owners,)), dma((owners,)),
            dma((owners,)), dma((owners,)), dma, dma,
            dma((owners,)), dma((owners,)),
        ],
        compiler_params=pltpu.CompilerParams(
            collective_id=0, has_side_effects=True, vmem_limit_bytes=48 << 20
        ),
    )(vectors, labels.reshape(1, count), sizes, heats)
    return out.reshape(count)


def solution(mesh):
    placed = (
        P(("grp", "blk", "rep", "sub"), None),
        P(("grp", "blk", "rep", "sub")),
        P("grp"),
        P("grp"),
    )
    return jax.shard_map(
        on_device,
        mesh=mesh,
        in_specs=placed,
        out_specs=P(("grp", "blk", "rep", "sub")),
        check_vma=False,
    )
```

profile of v0, /device:TPU:0, one launch (start us, length us, event | category | flops | bytes accessed | tf_op | source)
XLA Modules:
  0.0 52.7 jit_solution(12222591675411629403)
XLA Ops:
  0.0 0.0 copy-start
  0.0 1.4 %copy-done = f32[512,768]{1,0:T(8,128)S(1)} copy-done((f32[512,768]{1,0:T(8,128)S(1)}, f32[512,768]{1,0:T(8,128)}, u32[]{:S(2)}) %copy-start) | copy-done | bytes 1572888
  1.4 0.0 copy-start.1
  1.4 0.7 %copy-done.1 = s32[512]{0:T(512)S(1)} copy-done((s32[512]{0:T(512)S(1)}, s32[512]{0:T(512)}, u32[]{:S(2)}) %copy-start.1) | copy-done | bytes 2072
  2.1 0.0 copy-start.2
  2.1 0.7 %copy-done.2 = s32[24]{0:T(128)S(1)} copy-done((s32[24]{0:T(128)S(1)}, s32[24]{0:T(128)}, u32[]{:S(2)}) %copy-start.2) | copy-done | bytes 120
  2.7 0.0 copy-start.3
  2.7 0.7 %copy-done.3 = f32[24]{0:T(128)S(1)} copy-done((f32[24]{0:T(128)S(1)}, f32[24]{0:T(128)}, u32[]{:S(2)}) %copy-start.3) | copy-done | bytes 120
  3.4 48.7 %shard_map.46 = f32[1,512]{1,0:T(1,128)S(1)} custom-call(f32[512,768]{1,0:T(8,128)S(1)} %copy-done, s32[1,512]{1,0:T(1,128)S(1)} %bitcast.3, s32[24]{0:T(128)S(1)} %copy-done.2, f32[24]{0:T(128)S(1)} %copy-done.3), custom_call_target="tpu_custom_call" | custom-call | tf_op jit(solution)/shard_map/pallas_call | solution.py:219
  52.1 0.6 %copy.6 = f32[512]{0:T(512)} copy(f32[512]{0:T(512)S(1)} %bitcast.2) | data formatting | bytes 4096
Async XLA Ops:
  0.0 1.4 %copy-start = (f32[512,768]{1,0:T(8,128)S(1)}, f32[512,768]{1,0:T(8,128)}, u32[]{:S(2)}) copy-start(f32[512,768]{1,0:T(8,128)} %x_ref.1) | copy-start | bytes 4718596
  1.4 0.7 %copy-start.1 = (s32[512]{0:T(512)S(1)}, s32[512]{0:T(512)}, u32[]{:S(2)}) copy-start(s32[512]{0:T(512)} %param.5) | copy-start | bytes 6148
  2.1 0.7 %copy-start.2 = (s32[24]{0:T(128)S(1)}, s32[24]{0:T(128)}, u32[]{:S(2)}) copy-start(s32[24]{0:T(128)} %sizes_ref.1) | copy-start | bytes 292
  2.7 0.7 %copy-start.3 = (f32[24]{0:T(128)S(1)}, f32[24]{0:T(128)}, u32[]{:S(2)}) copy-start(f32[24]{0:T(128)} %heats_ref.1) | copy-start | bytes 292
where the time goes:
time: 52.8 us; the launch traced here: 52.7 us
  Pallas kernels  48.7 us (92%)
  local copies, waits for them, and re-layouts  3.98 us (8%)
    pallas_call x1, Pallas kernels, on_device(): pl.pallas_call(functools.partial(kernel, n_blk, n_rep, n_sub, slots), out...  48.7 us
    unnamed x9, local copies, waits for them, and re-layouts  3.98 us

commit v1 on v0

v1 whole, which is shorter than its diff:
```python
import functools

import jax
import jax.numpy as jnp
from jax import lax
from jax.experimental import pallas as pl
from jax.experimental.pallas import tpu as pltpu
from jax.sharding import PartitionSpec as P

D = 768
GROUPS_EACH_PEER = 3
ORDER = (0, 7, 6, 5, 4, 3, 2, 1)
LOADS = 4
MESH = pl.DeviceIdType.MESH
F32 = jnp.float32
BF16 = jnp.bfloat16


def kernel(
    n_blk, n_rep, n_sub, slots,
    x_hbm, label_ref, sizes_ref, heats_ref, out_ref,
    x_ref, unit, out_rows, out_tags, rows, tags, sums, back_out, back_in,
    load_sem, row_send, row_recv, tag_send, tag_recv, fwd_send, fwd_recv,
    fwd_tag_send, fwd_tag_recv, back_send, back_recv,
):
    owners = n_blk * n_rep
    bits = owners.bit_length() - 1
    parts = min(owners, len(ORDER))
    per = owners // parts
    span = per * slots
    count = x_ref.shape[0]
    me = lax.axis_index("blk") * n_rep + lax.axis_index("rep")
    sibling = {"sub": 1 - lax.axis_index("sub")}
    piece = count // LOADS

    def load(c):
        at = pl.ds(c * piece, piece)
        return pltpu.make_async_copy(x_hbm.at[at], x_ref.at[at], load_sem.at[c])

    for c in range(LOADS):
        load(c).start()

    def peer(k):
        o = 0
        for b in range(bits):
            o = o + lax.rem(lax.rem(me // 2**b, 2) + (k // 2**b) % 2, 2) * 2**b
        return o

    def device(owner):
        return {"blk": owner // n_rep, "rep": lax.rem(owner, n_rep)}

    def each(p, body):
        def step(q, carry):
            body(p * per + q, peer(ORDER[p] * per + q))
            return carry

        first = 1 if p == 0 else 0
        if per == 1:
            if not first:
                step(0, 0)
        else:
            lax.fori_loop(first, per, step, 0)

    def peers(body):
        for p in range(parts):
            each(p, body)

    barrier = pltpu.get_barrier_semaphore()
    peers(lambda n, o: pl.semaphore_signal(barrier, inc=1, device_id=device(o), device_id_type=MESH))
    pl.semaphore_signal(barrier, inc=1, device_id=sibling, device_id_type=MESH)

    labels = label_ref[...]
    owner_range = lax.broadcasted_iota(jnp.int32, (owners, count), 0) * GROUPS_EACH_PEER
    local = labels - owner_range
    mine_owner = (local >= 0) & (local < GROUPS_EACH_PEER)
    upper = (
        lax.broadcasted_iota(jnp.int32, (count, count), 0)
        < lax.broadcasted_iota(jnp.int32, (count, count), 1)
    )
    before = jnp.dot(
        jnp.where(mine_owner, 1.0, 0.0).astype(BF16),
        jnp.where(upper, 1.0, 0.0).astype(BF16),
        preferred_element_type=F32,
    )
    rank = jnp.sum(jnp.where(mine_owner, before, 0.0), axis=0, keepdims=True).astype(jnp.int32)
    first = jnp.sum(jnp.where(mine_owner, owner_range, 0), axis=0, keepdims=True)
    member = labels - first
    code = first * 256 + rank
    slot_range = lax.broadcasted_iota(jnp.int32, (slots, count), 0)
    wide_range = lax.broadcasted_iota(jnp.int32, (128, count), 0)
    tag_range = lax.broadcasted_iota(jnp.int32, (8, count), 0)
    tag_table = jnp.where(
        tag_range == GROUPS_EACH_PEER,
        (member + 1).astype(F32),
        jnp.where(tag_range == member, 1.0, 0.0),
    ).astype(BF16)

    def picked(owner, slot):
        return jnp.where(slot + owner * (GROUPS_EACH_PEER * 256) == code, 1.0, 0.0).astype(BF16)

    def tags_for(owner):
        return lax.dot_general(
            tag_table, picked(owner, wide_range), (((1,), (1,)), ((), ())),
            preferred_element_type=F32,
        )

    def rows_for(owner):
        return jnp.dot(
            picked(owner, slot_range), unit[...], preferred_element_type=F32
        ).astype(BF16)

    def normalise(c):
        load(c).wait()
        x = x_ref[c * piece : (c + 1) * piece]
        squares = jnp.sum(x * x, axis=1, keepdims=True)
        unit[c * piece : (c + 1) * piece] = (x * lax.rsqrt(squares + 1e-06)).astype(BF16)

    for c in range(LOADS):
        normalise(c)

    def row_copy(n, o):
        return pltpu.make_async_remote_copy(
            src_ref=out_rows.at[n], dst_ref=rows.at[0, n],
            send_sem=row_send.at[n], recv_sem=row_recv.at[n],
            device_id=device(o), device_id_type=MESH,
        )

    def tag_copy(n, o):
        return pltpu.make_async_remote_copy(
            src_ref=out_tags.at[n], dst_ref=tags.at[0, n],
            send_sem=tag_send.at[n], recv_sem=tag_recv.at[n],
            device_id=device(o), device_id_type=MESH,
        )

    def back_copy(n, o):
        return pltpu.make_async_remote_copy(
            src_ref=back_out.at[n], dst_ref=back_in.at[n],
            send_sem=back_send.at[n], recv_sem=back_recv.at[n],
            device_id=device(o), device_id_type=MESH,
        )

    def forward(n):
        return pltpu.make_async_remote_copy(
            src_ref=rows.at[0, n], dst_ref=rows.at[1, n],
            send_sem=fwd_send.at[n], recv_sem=fwd_recv.at[n],
            device_id=sibling, device_id_type=MESH,
        )

    def send_tags(n, o):
        out_tags[n] = tags_for(o)
        tag_copy(n, o).start()

    def send_rows(n, o):
        out_rows[n] = rows_for(o)
        row_copy(n, o).start()

    starting = [p for p in range(1, parts)] + [0]
    for turn, p in enumerate(starting):
        if turn == 0 and parts > 1:
            def first_rows(n, o):
                out_rows[n] = rows_for(o)

            each(p, first_rows)
            pl.semaphore_wait(barrier, owners)
            each(p, lambda n, o: row_copy(n, o).start())
            peers(send_tags)
            tags[0, 0] = tags_for(me)
        else:
            each(p, send_rows)
    rows[0, 0] = rows_for(me)
    forward(0).start()

    peers(lambda n, o: tag_copy(n, o).wait_recv())
    forward_tags = pltpu.make_async_remote_copy(
        src_ref=tags.at[0], dst_ref=tags.at[1],
        send_sem=fwd_tag_send, recv_sem=fwd_tag_recv,
        device_id=sibling, device_id_type=MESH,
    )
    forward_tags.start()

    hot = jnp.concatenate([tags[0, n][:, :slots] for n in range(owners)], axis=1)
    heat = jnp.zeros_like(hot[0:1])
    size = jnp.zeros_like(heat)
    for g in range(GROUPS_EACH_PEER):
        at = me * GROUPS_EACH_PEER + g
        heat = heat + hot[g : g + 1] * heats_ref[at]
        size = jnp.where(hot[g : g + 1] > 0.5, sizes_ref[at].astype(F32), size)
    valid = heat > 0.0
    inverse = 1.0 / jnp.where(valid, heat, 1.0)
    offset = inverse - jnp.log(jnp.where(valid, size, 1.0))
    tag_row = hot[GROUPS_EACH_PEER : GROUPS_EACH_PEER + 1]
    forward_tags.wait_recv()

    def tag_column(s, lo, hi):
        return jnp.concatenate(
            [
                tags[s, n].T[:slots, GROUPS_EACH_PEER : GROUPS_EACH_PEER + 1]
                for n in range(lo * per, hi * per)
            ],
            axis=0,
        )

    def block(s, lo, hi):
        return rows[s, lo * per : hi * per].reshape((hi - lo) * span, D)

    def column(s, j0, j1, i0, i1):
        cosine = lax.dot_general(
            block(s, j0, j1), block(0, i0, i1), (((1,), (1,)), ((), ())),
            preferred_element_type=F32,
        )
        at = slice(i0 * span, i1 * span)
        weight = jnp.where(
            tag_column(s, j0, j1) == tag_row[:, at],
            jnp.exp((cosine - 1.0) * inverse[:, at]),
            0.0,
        )
        return jnp.sum(weight, axis=0, keepdims=True)

    def arrive(n, o):
        row_copy(n, o).wait_recv()
        forward(n).start()

    sums[...] = jnp.zeros_like(sums)
    back_out[...] = jnp.zeros_like(back_out)
    late = []
    for p in range(parts):
        each(p, arrive)
        upto = slice(0, (p + 1) * span)
        sums[:, upto] += column(0, p, p + 1, 0, p + 1)
        if p:
            late.append(column(0, 0, p, p, p + 1) + column(1, 0, p, p, p + 1))
        else:
            late.append(jnp.zeros((1, span), F32))
            forward(0).wait_recv()
        each(p, lambda n, o: forward(n).wait_recv())
        sums[:, upto] += column(1, p, p + 1, 0, p + 1)

    total = sums[...] + jnp.concatenate(late, axis=1)
    scores = jnp.where(valid, offset + jnp.log(jnp.where(valid, total, 1.0)), 0.0)
    for n in range(owners):
        back_out[n, 0:1, 0:slots] = scores[:, n * slots : (n + 1) * slots]
    peers(lambda n, o: back_copy(n, o).start())
    back_in[0] = back_out[0]

    def drain(n, o):
        tag_copy(n, o).wait_send()
        row_copy(n, o).wait_send()
        forward(n).wait_send()

    peers(drain)
    forward(0).wait_send()
    forward_tags.wait_send()
    spread = jnp.where(wide_range == rank, 1.0, 0.0)

    peers(lambda n, o: back_copy(n, o).wait_recv())
    table = back_in[:, 0, :]
    found = jnp.dot(table, spread, precision=lax.Precision.HIGHEST, preferred_element_type=F32)
    out = jnp.where(first == me * GROUPS_EACH_PEER, found[0:1], 0.0)
    for n in range(1, owners):
        o = peer(ORDER[n // per] * per + n % per)
        out = jnp.where(first == o * GROUPS_EACH_PEER, found[n : n + 1], out)
    out_ref[...] = out
    peers(lambda n, o: back_copy(n, o).wait_send())


def on_device(vectors, labels, sizes, heats):
    count = vectors.shape[0]
    n_blk, n_rep, n_sub = (lax.axis_size(a) for a in ("blk", "rep", "sub"))
    owners = n_blk * n_rep
    share = count // owners
    slots = -(-(share + share // 2) // 16) * 16
    dma = pltpu.SemaphoreType.DMA
    out = pl.pallas_call(
        functools.partial(kernel, n_blk, n_rep, n_sub, slots),
        out_shape=jax.ShapeDtypeStruct((1, count), F32),
        in_specs=[
            pl.BlockSpec(memory_space=pltpu.HBM),
            pl.BlockSpec(memory_space=pltpu.VMEM),
            pl.BlockSpec(memory_space=pltpu.SMEM),
            pl.BlockSpec(memory_space=pltpu.SMEM),
        ],
        out_specs=pl.BlockSpec(memory_space=pltpu.VMEM),
        scratch_shapes=[
            pltpu.VMEM((count, D), F32),
            pltpu.VMEM((count, D), BF16),
            pltpu.VMEM((owners, slots, D), BF16),
            pltpu.VMEM((owners, 8, 128), F32),
            pltpu.VMEM((n_sub, owners, slots, D), BF16),
            pltpu.VMEM((n_sub, owners, 8, 128), F32),
            pltpu.VMEM((1, owners * slots), F32),
            pltpu.VMEM((owners, 8, 128), F32),
            pltpu.VMEM((owners, 8, 128), F32),
            dma((LOADS,)),
            dma((owners,)), dma((owners,)), dma((owners,)), dma((owners,)),
            dma((owners,)), dma((owners,)), dma, dma,
            dma((owners,)), dma((owners,)),
        ],
        compiler_params=pltpu.CompilerParams(
            collective_id=0, has_side_effects=True, vmem_limit_bytes=48 << 20
        ),
    )(vectors, labels.reshape(1, count), sizes, heats)
    return out.reshape(count)


def solution(mesh):
    placed = (
        P(("grp", "blk", "rep", "sub"), None),
        P(("grp", "blk", "rep", "sub")),
        P("grp"),
        P("grp"),
    )
    return jax.shard_map(
        on_device,
        mesh=mesh,
        in_specs=placed,
        out_specs=P(("grp", "blk", "rep", "sub")),
        check_vma=False,
    )
```

time: 52.8 us -> 50.4 us (0.955)
  Pallas kernels: 48.7 us -> 46.2 us
    pallas_call x1, Pallas kernels: 48.7 us -> 46.2 us  [on_device(): pl.pallas_call(functools.partial(kernel, n_blk, n_rep, n_sub, slots), out...]
where the time goes in v1:
time: 50.4 us; the launch traced here: 50.2 us
  Pallas kernels  46.2 us (92%)
  local copies, waits for them, and re-layouts  3.98 us (8%)
    pallas_call x1, Pallas kernels, on_device(): pl.pallas_call(functools.partial(kernel, n_blk, n_rep, n_sub, slots), out...  46.2 us
    unnamed x9, local copies, waits for them, and re-layouts  3.98 us

profile of v1, /device:TPU:0, one launch (start us, length us, event | category | flops | bytes accessed | tf_op | source)
XLA Modules:
  0.0 50.2 jit_solution(8039483645933487546)
XLA Ops:
  0.0 0.0 copy-start
  0.0 1.4 %copy-done = f32[512,768]{1,0:T(8,128)S(1)} copy-done((f32[512,768]{1,0:T(8,128)S(1)}, f32[512,768]{1,0:T(8,128)}, u32[]{:S(2)}) %copy-start) | copy-done | bytes 1572888
  1.4 0.0 copy-start.1
  1.4 0.7 %copy-done.1 = s32[512]{0:T(512)S(1)} copy-done((s32[512]{0:T(512)S(1)}, s32[512]{0:T(512)}, u32[]{:S(2)}) %copy-start.1) | copy-done | bytes 2072
  2.1 0.0 copy-start.2
  2.1 0.7 %copy-done.2 = s32[24]{0:T(128)S(1)} copy-done((s32[24]{0:T(128)S(1)}, s32[24]{0:T(128)}, u32[]{:S(2)}) %copy-start.2) | copy-done | bytes 120
  2.7 0.0 copy-start.3
  2.7 0.7 %copy-done.3 = f32[24]{0:T(128)S(1)} copy-done((f32[24]{0:T(128)S(1)}, f32[24]{0:T(128)}, u32[]{:S(2)}) %copy-start.3) | copy-done | bytes 120
  3.4 46.2 %shard_map.46 = f32[1,512]{1,0:T(1,128)S(1)} custom-call(f32[512,768]{1,0:T(8,128)S(1)} %copy-done, s32[1,512]{1,0:T(1,128)S(1)} %bitcast.3, s32[24]{0:T(128)S(1)} %copy-done.2, f32[24]{0:T(128)S(1)} %copy-done.3), custom_call_target="tpu_custom_call" | custom-call | tf_op jit(solution)/shard_map/pallas_call | solution.py:273
  49.6 0.6 %copy.6 = f32[512]{0:T(512)} copy(f32[512]{0:T(512)S(1)} %bitcast.2) | data formatting | bytes 4096
Async XLA Ops:
  0.0 1.4 %copy-start = (f32[512,768]{1,0:T(8,128)S(1)}, f32[512,768]{1,0:T(8,128)}, u32[]{:S(2)}) copy-start(f32[512,768]{1,0:T(8,128)} %x_hbm.1) | copy-start | bytes 4718596
  1.4 0.7 %copy-start.1 = (s32[512]{0:T(512)S(1)}, s32[512]{0:T(512)}, u32[]{:S(2)}) copy-start(s32[512]{0:T(512)} %param.5) | copy-start | bytes 6148
  2.1 0.7 %copy-start.2 = (s32[24]{0:T(128)S(1)}, s32[24]{0:T(128)}, u32[]{:S(2)}) copy-start(s32[24]{0:T(128)} %sizes_ref.1) | copy-start | bytes 292
  2.7 0.7 %copy-start.3 = (f32[24]{0:T(128)S(1)}, f32[24]{0:T(128)}, u32[]{:S(2)}) copy-start(f32[24]{0:T(128)} %heats_ref.1) | copy-start | bytes 292

commit v2 on v1

--- a/solution.py
+++ b/solution.py
@@ -9,7 +9,7 @@
 
 D = 768
 GROUPS_EACH_PEER = 3
-ORDER = (0, 7, 6, 5, 4, 3, 2, 1)
+ORDERS = ((0, 4, 1, 5, 2, 6, 3, 7), (0, 1, 4, 2, 5, 3, 6, 7))
 LOADS = 4
 MESH = pl.DeviceIdType.MESH
 F32 = jnp.float32
@@ -25,12 +25,13 @@
 ):
     owners = n_blk * n_rep
     bits = owners.bit_length() - 1
-    parts = min(owners, len(ORDER))
+    parts = min(owners, len(ORDERS[0]))
     per = owners // parts
     span = per * slots
     count = x_ref.shape[0]
     me = lax.axis_index("blk") * n_rep + lax.axis_index("rep")
-    sibling = {"sub": 1 - lax.axis_index("sub")}
+    sub = lax.axis_index("sub")
+    sibling = {"sub": 1 - sub}
     piece = count // LOADS
 
     def load(c):
@@ -43,15 +44,19 @@
     def peer(k):
         o = 0
         for b in range(bits):
-            o = o + lax.rem(lax.rem(me // 2**b, 2) + (k // 2**b) % 2, 2) * 2**b
+            o = o + lax.rem(lax.rem(me // 2**b, 2) + lax.rem(k // 2**b, 2), 2) * 2**b
         return o
 
     def device(owner):
         return {"blk": owner // n_rep, "rep": lax.rem(owner, n_rep)}
 
+    def relative(p):
+        near, far = ORDERS[0][p], ORDERS[1][p]
+        return near + sub * (far - near)
+
     def each(p, body):
         def step(q, carry):
-            body(p * per + q, peer(ORDER[p] * per + q))
+            body(p * per + q, peer(relative(p) * per + q))
             return carry
 
         first = 1 if p == 0 else 0
@@ -216,6 +221,11 @@
         )
         return jnp.sum(weight, axis=0, keepdims=True)
 
+    def arrive_sibling(p):
+        if p == 0:
+            forward(0).wait_recv()
+        each(p, lambda n, o: forward(n).wait_recv())
+
     def arrive(n, o):
         row_copy(n, o).wait_recv()
         forward(n).start()
@@ -226,14 +236,18 @@
     for p in range(parts):
         each(p, arrive)
         upto = slice(0, (p + 1) * span)
-        sums[:, upto] += column(0, p, p + 1, 0, p + 1)
+        part = column(0, p, p + 1, 0, p + 1)
+        extra = jnp.zeros((1, span), F32)
         if p:
-            late.append(column(0, 0, p, p, p + 1) + column(1, 0, p, p, p + 1))
-        else:
-            late.append(jnp.zeros((1, span), F32))
-            forward(0).wait_recv()
-        each(p, lambda n, o: forward(n).wait_recv())
-        sums[:, upto] += column(1, p, p + 1, 0, p + 1)
+            extra = extra + column(0, 0, p, p, p + 1)
+            if p > 1:
+                extra = extra + column(1, 0, p - 1, p, p + 1)
+            arrive_sibling(p - 1)
+            part = part + column(1, p - 1, p, 0, p + 1)
+        late.append(extra)
+        sums[:, upto] += part
+    arrive_sibling(parts - 1)
+    sums[...] += column(1, parts - 1, parts, 0, parts)
 
     total = sums[...] + jnp.concatenate(late, axis=1)
     scores = jnp.where(valid, offset + jnp.log(jnp.where(valid, total, 1.0)), 0.0)
@@ -257,7 +271,7 @@
     found = jnp.dot(table, spread, precision=lax.Precision.HIGHEST, preferred_element_type=F32)
     out = jnp.where(first == me * GROUPS_EACH_PEER, found[0:1], 0.0)
     for n in range(1, owners):
-        o = peer(ORDER[n // per] * per + n % per)
+        o = peer(relative(n // per) * per + n % per)
         out = jnp.where(first == o * GROUPS_EACH_PEER, found[n : n + 1], out)
     out_ref[...] = out
     peers(lambda n, o: back_copy(n, o).wait_send())

time: 50.4 us -> 46.4 us (0.921)
  Pallas kernels: 46.2 us -> 42.3 us
    pallas_call x1, Pallas kernels: 46.2 us -> 42.3 us  [on_device(): pl.pallas_call(functools.partial(kernel, n_blk, n_rep, n_sub, slots), out...]
where the time goes in v2:
time: 46.4 us; the launch traced here: 46.3 us
  Pallas kernels  42.3 us (91%)
  local copies, waits for them, and re-layouts  3.98 us (9%)
    pallas_call x1, Pallas kernels, on_device(): pl.pallas_call(functools.partial(kernel, n_blk, n_rep, n_sub, slots), out...  42.3 us
    unnamed x9, local copies, waits for them, and re-layouts  3.98 us

profile of v2, /device:TPU:0, one launch (start us, length us, event | category | flops | bytes accessed | tf_op | source)
XLA Modules:
  0.0 46.3 jit_solution(9685552699449633167)
XLA Ops:
  0.0 0.0 copy-start
  0.0 1.4 %copy-done = f32[512,768]{1,0:T(8,128)S(1)} copy-done((f32[512,768]{1,0:T(8,128)S(1)}, f32[512,768]{1,0:T(8,128)}, u32[]{:S(2)}) %copy-start) | copy-done | bytes 1572888
  1.4 0.0 copy-start.1
  1.4 0.7 %copy-done.1 = s32[512]{0:T(512)S(1)} copy-done((s32[512]{0:T(512)S(1)}, s32[512]{0:T(512)}, u32[]{:S(2)}) %copy-start.1) | copy-done | bytes 2072
  2.1 0.0 copy-start.2
  2.1 0.7 %copy-done.2 = s32[24]{0:T(128)S(1)} copy-done((s32[24]{0:T(128)S(1)}, s32[24]{0:T(128)}, u32[]{:S(2)}) %copy-start.2) | copy-done | bytes 120
  2.7 0.0 copy-start.3
  2.7 0.7 %copy-done.3 = f32[24]{0:T(128)S(1)} copy-done((f32[24]{0:T(128)S(1)}, f32[24]{0:T(128)}, u32[]{:S(2)}) %copy-start.3) | copy-done | bytes 120
  3.4 42.3 %shard_map.46 = f32[1,512]{1,0:T(1,128)S(1)} custom-call(f32[512,768]{1,0:T(8,128)S(1)} %copy-done, s32[1,512]{1,0:T(1,128)S(1)} %bitcast.3, s32[24]{0:T(128)S(1)} %copy-done.2, f32[24]{0:T(128)S(1)} %copy-done.3), custom_call_target="tpu_custom_call" | custom-call | tf_op jit(solution)/shard_map/pallas_call | solution.py:287
  45.7 0.6 %copy.6 = f32[512]{0:T(512)} copy(f32[512]{0:T(512)S(1)} %bitcast.2) | data formatting | bytes 4096
Async XLA Ops:
  0.0 1.4 %copy-start = (f32[512,768]{1,0:T(8,128)S(1)}, f32[512,768]{1,0:T(8,128)}, u32[]{:S(2)}) copy-start(f32[512,768]{1,0:T(8,128)} %x_hbm.1) | copy-start | bytes 4718596
  1.4 0.7 %copy-start.1 = (s32[512]{0:T(512)S(1)}, s32[512]{0:T(512)}, u32[]{:S(2)}) copy-start(s32[512]{0:T(512)} %param.5) | copy-start | bytes 6148
  2.1 0.7 %copy-start.2 = (s32[24]{0:T(128)S(1)}, s32[24]{0:T(128)}, u32[]{:S(2)}) copy-start(s32[24]{0:T(128)} %sizes_ref.1) | copy-start | bytes 292
  2.7 0.7 %copy-start.3 = (f32[24]{0:T(128)S(1)}, f32[24]{0:T(128)}, u32[]{:S(2)}) copy-start(f32[24]{0:T(128)} %heats_ref.1) | copy-start | bytes 292

commit v3 on v2

--- a/solution.py
+++ b/solution.py
@@ -168,10 +168,11 @@
             each(p, first_rows)
             pl.semaphore_wait(barrier, owners)
             each(p, lambda n, o: row_copy(n, o).start())
+        else:
+            each(p, send_rows)
+        if turn == min(1, parts - 2):
             peers(send_tags)
             tags[0, 0] = tags_for(me)
-        else:
-            each(p, send_rows)
     rows[0, 0] = rows_for(me)
     forward(0).start()
 
@@ -233,21 +234,19 @@
     sums[...] = jnp.zeros_like(sums)
     back_out[...] = jnp.zeros_like(back_out)
     late = []
-    for p in range(parts):
-        each(p, arrive)
-        upto = slice(0, (p + 1) * span)
-        part = column(0, p, p + 1, 0, p + 1)
-        extra = jnp.zeros((1, span), F32)
-        if p:
-            extra = extra + column(0, 0, p, p, p + 1)
-            if p > 1:
-                extra = extra + column(1, 0, p - 1, p, p + 1)
-            arrive_sibling(p - 1)
-            part = part + column(1, p - 1, p, 0, p + 1)
+    step = -(-parts // 4)
+    for lo in range(0, parts, step):
+        hi = lo + step
+        for p in range(lo, hi):
+            each(p, arrive)
+        part = column(0, lo, hi, 0, hi)
+        extra = jnp.zeros((1, (hi - lo) * span), F32)
+        if lo:
+            extra = column(0, 0, lo, lo, hi) + column(1, 0, lo, lo, hi)
         late.append(extra)
-        sums[:, upto] += part
-    arrive_sibling(parts - 1)
-    sums[...] += column(1, parts - 1, parts, 0, parts)
+        for p in range(lo, hi):
+            arrive_sibling(p)
+        sums[:, 0 : hi * span] += part + column(1, lo, hi, 0, hi)
 
     total = sums[...] + jnp.concatenate(late, axis=1)
     scores = jnp.where(valid, offset + jnp.log(jnp.where(valid, total, 1.0)), 0.0)
@@ -310,7 +309,7 @@
             dma((owners,)), dma((owners,)),
         ],
         compiler_params=pltpu.CompilerParams(
-            collective_id=0, has_side_effects=True, vmem_limit_bytes=48 << 20
+            collective_id=0, has_side_effects=True, vmem_limit_bytes=64 << 20
         ),
     )(vectors, labels.reshape(1, count), sizes, heats)
     return out.reshape(count)

time: 46.4 us -> 43.2 us (0.931)
  local copies, waits for them, and re-layouts: 3.98 us -> 1.26 us
  Pallas kernels: 42.3 us -> 41.7 us
    unnamed x9 -> x1, local copies, waits for them, and re-layouts: 3.98 us -> 1.26 us
    pallas_call x1, Pallas kernels: 42.3 us -> 41.7 us  [on_device(): pl.pallas_call(functools.partial(kernel, n_blk, n_rep, n_sub, slots), out...]
where the time goes in v3:
time: 43.2 us; the launch traced here: 43 us
  Pallas kernels  41.7 us (97%)
  local copies, waits for them, and re-layouts  1.26 us (3%)
    pallas_call x1, Pallas kernels, on_device(): pl.pallas_call(functools.partial(kernel, n_blk, n_rep, n_sub, slots), out...  41.7 us
    unnamed x1, local copies, waits for them, and re-layouts  1.26 us

profile of v3, /device:TPU:0, one launch (start us, length us, event | category | flops | bytes accessed | tf_op | source)
XLA Modules:
  0.0 43.0 jit_solution(13753218141946552863)
XLA Ops:
  0.0 41.7 %shard_map.46 = f32[1,512]{1,0:T(1,128)} custom-call(f32[512,768]{1,0:T(8,128)} %x_hbm.1, s32[1,512]{1,0:T(1,128)} %bitcast.3, s32[24]{0:T(128)} %sizes_ref.1, f32[24]{0:T(128)} %heats_ref.1), custom_call_target="tpu_custom_call" | custom-call | tf_op jit(solution)/shard_map/pallas_call | solution.py:286
  41.7 1.3 %copy.6 = f32[512]{0:T(512)} copy(f32[512]{0:T(512)} %bitcast.2) | data formatting | bytes 4096

commit v4 on v3

--- a/solution.py
+++ b/solution.py
@@ -120,6 +120,11 @@
         squares = jnp.sum(x * x, axis=1, keepdims=True)
         unit[c * piece : (c + 1) * piece] = (x * lax.rsqrt(squares + 1e-06)).astype(BF16)
 
+    def make_tags(n, o):
+        out_tags[n] = tags_for(o)
+
+    peers(make_tags)
+    tags[0, 0] = tags_for(me)
     for c in range(LOADS):
         normalise(c)
 
@@ -151,10 +156,6 @@
             device_id=sibling, device_id_type=MESH,
         )
 
-    def send_tags(n, o):
-        out_tags[n] = tags_for(o)
-        tag_copy(n, o).start()
-
     def send_rows(n, o):
         out_rows[n] = rows_for(o)
         row_copy(n, o).start()
@@ -167,12 +168,10 @@
 
             each(p, first_rows)
             pl.semaphore_wait(barrier, owners)
+            peers(lambda n, o: tag_copy(n, o).start())
             each(p, lambda n, o: row_copy(n, o).start())
         else:
             each(p, send_rows)
-        if turn == min(1, parts - 2):
-            peers(send_tags)
-            tags[0, 0] = tags_for(me)
     rows[0, 0] = rows_for(me)
     forward(0).start()
 

time: 43.2 us -> 43 us (level)
  no operation moved by 1% of the time
where the time goes in v4:
time: 43 us; the launch traced here: 42.8 us
  Pallas kernels  41.5 us (97%)
  local copies, waits for them, and re-layouts  1.26 us (3%)
    pallas_call x1, Pallas kernels, on_device(): pl.pallas_call(functools.partial(kernel, n_blk, n_rep, n_sub, slots), out...  41.5 us
    unnamed x1, local copies, waits for them, and re-layouts  1.26 us

profile of v4, /device:TPU:0, one launch (start us, length us, event | category | flops | bytes accessed | tf_op | source)
XLA Modules:
  0.0 42.8 jit_solution(5184711297244059247)
XLA Ops:
  0.0 41.5 %shard_map.46 = f32[1,512]{1,0:T(1,128)} custom-call(f32[512,768]{1,0:T(8,128)} %x_hbm.1, s32[1,512]{1,0:T(1,128)} %bitcast.3, s32[24]{0:T(128)} %sizes_ref.1, f32[24]{0:T(128)} %heats_ref.1), custom_call_target="tpu_custom_call" | custom-call | tf_op jit(solution)/shard_map/pallas_call | solution.py:285
  41.5 1.3 %copy.6 = f32[512]{0:T(512)} copy(f32[512]{0:T(512)} %bitcast.2) | data formatting | bytes 4096
